TPU v7x, 32 devices: a whole 2x2x4 slice. The times are simulated.
32 devices in a mesh: wn: 4 (over y, core), sp: 8 (over z, x).
Axes of the slice: x: 2, y: 2, z: 4, core: 2. Of those that a mesh axis runs over, the one named last changes fastest.
Arguments:
- random_slabs: float32 [8, 3, 512, 1024], P(None, None, 'wn', 'sp'), may hold values from -6 to 6
- stress: float32 [6, 512], P(None, 'wn'), may hold values from -0.8 to 2, as said below
- profile: float32 [512], P('wn'), may hold values from 0.2 to 1.2
Outputs:
- inflow: float32 [8, 3, 512, 1024], P(None, None, 'wn', 'sp')
Inputs may be any that keep to these rules, and one draw needn't show every extreme that they name: R11, R22 and R33 are positive, and each off-diagonal stress is at most 0.4 times the square root of the product of its two diagonal stresses in magnitude.
All inputs are finite; a program needn't handle non-finite values.
Results may differ from a plain program's by a relative error of at most 0.0003.
Values sent between devices are 32-bit elements; how exact they have to be, the bound alone decides.
A program may use at most 128 MiB of HBM per device.

v0:
```python
import jax
import jax.numpy as jnp
from jax import lax
from jax.sharding import PartitionSpec as P

H = 64


epsilon = 1e-06


def with_halo(block, sides, width, periodic):
    for axis, dim in sides:
        count = lax.axis_size(axis)
        forward = [(i, i + 1) for i in range(count - 1)]
        if periodic:
            forward.append((count - 1, 0))
        backward = [(target, source) for source, target in forward]
        low = lax.ppermute(
            lax.slice_in_dim(block, block.shape[dim] - width, None, axis=dim), axis, forward
        )
        high = lax.ppermute(lax.slice_in_dim(block, 0, width, axis=dim), axis, backward)
        block = jnp.concatenate([low, block, high], axis=dim)
    return block


def band_matrix(reach):
    width = 2 * reach
    offset = jnp.arange(-reach, reach + 1).astype(jnp.float32)
    scale_len = reach / 2.0
    norming = jnp.sqrt(jnp.sum(jnp.exp(-jnp.pi * offset * offset / (scale_len * scale_len))))
    source = jnp.arange(2 * width)[:, None]
    target = jnp.arange(width)[None, :]
    lag = (source - target - reach).astype(jnp.float32)
    values = jnp.exp(-jnp.pi * lag * lag / (2.0 * scale_len * scale_len)) / norming
    return jnp.where(jnp.abs(lag) <= reach, values, 0.0)


def filter_last(padded, reach):
    width = 2 * reach
    band = band_matrix(reach)
    lead = padded.shape[:-1]
    blocks = padded.reshape(lead + (padded.shape[-1] // width, width))
    upper = jnp.matmul(blocks[..., :-1, :], band[:width], precision=lax.Precision.HIGHEST)
    lower = jnp.matmul(blocks[..., 1:, :], band[width:], precision=lax.Precision.HIGHEST)
    return (upper + lower).reshape(lead + (padded.shape[-1] - width,))


def filter_rows(padded, reach):
    width = 2 * reach
    band = band_matrix(reach)
    steps_n, comps, length, cols = padded.shape
    blocks = padded.reshape(steps_n, comps, length // width, width, cols)
    upper = jnp.einsum(
        "scbjz,ji->scbiz", blocks[:, :, :-1], band[:width], precision=lax.Precision.HIGHEST
    )
    lower = jnp.einsum(
        "scbjz,ji->scbiz", blocks[:, :, 1:], band[width:], precision=lax.Precision.HIGHEST
    )
    return (upper + lower).reshape(steps_n, comps, length - width, cols)


def lund(scaled, stress, profile):
    chol_xx = jnp.sqrt(stress[0])
    chol_yx = stress[3] / chol_xx
    chol_yy = jnp.sqrt(stress[1] - chol_yx * chol_yx)
    chol_zx = stress[4] / chol_xx
    chol_zy = (stress[5] - chol_yx * chol_zx) / chol_yy
    chol_zz = jnp.sqrt(stress[2] - chol_zx * chol_zx - chol_zy * chol_zy)
    first = profile[:, None] + chol_xx[:, None] * scaled[:, 0]
    second = chol_yx[:, None] * scaled[:, 0] + chol_yy[:, None] * scaled[:, 1]
    third = (
        chol_zx[:, None] * scaled[:, 0]
        + chol_zy[:, None] * scaled[:, 1]
        + chol_zz[:, None] * scaled[:, 2]
    )
    return jnp.stack([first, second, third], axis=1)


def body(random_slabs, stress, profile):
    padded = with_halo(random_slabs, (("wn", 2),), H, False)
    normal_pass = filter_rows(padded, H)
    span_total = lax.axis_size("sp") * normal_pass.shape[3]
    wrapped = with_halo(normal_pass, (("sp", 3),), H, True)
    filtered = filter_last(wrapped, H)
    sum_first, sum_second = lax.psum(
        (jnp.sum(filtered, axis=-1), jnp.sum(filtered * filtered, axis=-1)), "sp"
    )
    row_mean = sum_first / span_total
    centred = filtered - row_mean[..., None]
    row_var = sum_second / span_total - row_mean * row_mean
    scaled = centred / jnp.sqrt(row_var[..., None] + epsilon)
    return lund(scaled, stress, profile)


def solution(mesh):
    return jax.shard_map(
        body,
        mesh=mesh,
        in_specs=(P(None, None, "wn", "sp"), P(None, "wn"), P("wn")),
        out_specs=P(None, None, "wn", "sp"),
        check_vma=False,
    )
```

profile of v0, /device:TPU:0, one launch (start us, length us, event | category | flops | bytes accessed | tf_op | source)
XLA Modules:
  0.0 97.1 jit_solution(5936294462483977575)
XLA Ops:
  0.0 0.0 copy-start
  0.0 2.8 %fusion.21 = (f32[8,3,64,128]{3,2,1,0:T(8,128)}, f32[8,3,64,128]{3,2,1,0:T(8,128)}) fusion(f32[8,3,128,128]{3,2,1,0:T(8,128)} %param.3), kind=kLoop, calls=%fused_computation.49 | loop fusion | bytes 3145728 | tf_op jit(solution)/shard_map/slice | solution.py:20
  2.8 2.4 %collective-permute-start = (f32[8,3,64,128]{3,2,1,0:T(8,128)}, f32[8,3,64,128]{3,2,1,0:T(8,128)S(1)}, u32[]{:S(2)}, u32[]{:S(2)}) collective-permute-start(f32[8,3,64,128]{3,2,1,0:T(8,128)} %get-tuple-element.18), channel_id=1, source_target_pairs={{0,8},{8,16},{16,24},{1,9},{9,17},{17,25},{2,10},{10,18},{18,26},{... | collective-permute-start | bytes 2359304 | tf_op jit(solution)/shard_map/ppermute | solution.py:19
  5.2 1.3 %collective-permute-start.1 = (f32[8,3,64,128]{3,2,1,0:T(8,128)}, f32[8,3,64,128]{3,2,1,0:T(8,128)S(1)}, u32[]{:S(2)}, u32[]{:S(2)}) collective-permute-start(f32[8,3,64,128]{3,2,1,0:T(8,128)} %get-tuple-element.19), channel_id=1, source_target_pairs={{8,0},{16,8},{24,16},{9,1},{17,9},{25,17},{10,2},{18,10},{26,18},{... | collective-permute-start | bytes 2359304 | tf_op jit(solution)/shard_map/ppermute | solution.py:22
  6.5 0.6 fusion.12
  7.8 0.1 fusion.9
  7.9 0.0 collective-permute-done
  7.9 3.8 %collective-permute-done.1 = f32[8,3,64,128]{3,2,1,0:T(8,128)S(1)} collective-permute-done((f32[8,3,64,128]{3,2,1,0:T(8,128)}, f32[8,3,64,128]{3,2,1,0:T(8,128)S(1)}, u32[]{:S(2)}, u32[]{:S(2)}) %collective-permute-start.1) | collective-permute-done | bytes 786464 | tf_op jit(solution)/shard_map/ppermute | solution.py:22
  11.7 0.0 copy-done
  11.7 0.2 pad_maximum_fusion
  11.9 2.7 %fusion.2 = f32[128,8,3,128]{0,3,2,1:T(8,128)S(1)} fusion(f32[8,3,2,128,128]{4,3,2,1,0:T(8,128)S(1)} %bitcast.90, f32[256,128]{1,0:T(8,128)S(1)} %fusion.9), kind=kOutput, calls=%fused_computation.7 | convolution fusion | flops 603979776 | bytes 3211264 | tf_op jit(solution)/shard_map/scbjz,ji->scbiz/dot_general | solution.py:57
  14.6 2.6 %add_bitcast_fusion = f32[8,3,128,128]{2,3,1,0:T(8,128)S(1)} fusion(f32[128,8,3,128]{0,3,2,1:T(8,128)S(1)} %fusion.2, f32[8,3,2,128,128]{4,3,2,1,0:T(8,128)S(1)} %bitcast.91, f32[256,128]{1,0:T(8,128)S(1)} %fusion.9), kind=kOutput, calls=%fused_computation.13 | convolution fusion | flops 604372992 | bytes 4784128 | tf_op jit(solution)/shard_map/scbjz,ji->scbiz/dot_general | solution.py:54
  17.2 0.0 copy-start.1
  17.2 0.2 fusion.20
  17.4 1.5 %collective-permute-start.2 = (f32[8,3,128,64]{2,3,1,0:T(8,128)S(1)}, f32[8,3,128,64]{2,3,1,0:T(8,128)S(1)}, u32[]{:S(2)}, u32[]{:S(2)}) collective-permute-start(f32[8,3,128,64]{2,3,1,0:T(8,128)S(1)} %get-tuple-element.16), channel_id=1, source_target_pairs={{0,1},{1,2},{2,3},{3,4},{4,5},{5,6},{6,7},{7,0},{8,9},{9,10},{10,1... | collective-permute-start | bytes 2359304 | tf_op jit(solution)/shard_map/ppermute | solution.py:19
  19.0 3.2 %collective-permute-start.3 = (f32[8,3,128,64]{2,3,1,0:T(8,128)S(1)}, f32[8,3,128,64]{2,3,1,0:T(8,128)S(1)}, u32[]{:S(2)}, u32[]{:S(2)}) collective-permute-start(f32[8,3,128,64]{2,3,1,0:T(8,128)S(1)} %get-tuple-element.17), channel_id=1, source_target_pairs={{1,0},{2,1},{3,2},{4,3},{5,4},{6,5},{7,6},{0,7},{9,8},{10,9},{11,1... | collective-permute-start | bytes 2359304 | tf_op jit(solution)/shard_map/ppermute | solution.py:22
  22.2 0.0 copy-done.1
  22.2 28.9 %collective-permute-done.2 = f32[8,3,128,64]{2,3,1,0:T(8,128)S(1)} collective-permute-done((f32[8,3,128,64]{2,3,1,0:T(8,128)S(1)}, f32[8,3,128,64]{2,3,1,0:T(8,128)S(1)}, u32[]{:S(2)}, u32[]{:S(2)}) %collective-permute-start.2) | collective-permute-done | bytes 786464 | tf_op jit(solution)/shard_map/ppermute | solution.py:19
  51.1 3.7 %collective-permute-done.3 = f32[8,3,128,64]{2,3,1,0:T(8,128)S(1)} collective-permute-done((f32[8,3,128,64]{2,3,1,0:T(8,128)S(1)}, f32[8,3,128,64]{2,3,1,0:T(8,128)S(1)}, u32[]{:S(2)}, u32[]{:S(2)}) %collective-permute-start.3) | collective-permute-done | bytes 786464 | tf_op jit(solution)/shard_map/ppermute | solution.py:22
  54.9 0.3 pad_maximum_fusion.1
  55.2 1.5 %fusion = f32[8,3,128,128]{2,3,1,0:T(8,128)S(1)} fusion(f32[8,3,128,2,128]{2,4,3,1,0:T(8,128)S(1)} %bitcast.88, f32[256,128]{1,0:T(8,128)S(1)} %fusion.9), kind=kOutput, calls=%fused_computation.3 | convolution fusion | flops 603979776 | bytes 3211264 | tf_op jit(solution)/shard_map/dot_general | solution.py:45
  56.7 1.8 %fusion.18 = (f32[8,3,128]{2,1,0:T(4,128)S(1)}, f32[8,3,128]{2,1,0:T(4,128)S(1)}, f32[8,3,128,128]{2,3,1,0:T(8,128)S(1)}) fusion(f32[8,3,128,128]{2,3,1,0:T(8,128)S(1)} %fusion, f32[256,128]{1,0:T(8,128)S(1)} %fusion.9, f32[8,3,128,2,128]{2,4,3,1,0:T(8,128)S(1)} %bitcast.89), kind=kOutput, calls=%fused_computation.47 | convolution fusion | flops 605546496 | bytes 4808704 | tf_op jit(solution)/shard_map/dot_general | solution.py:44
  58.5 35.9 %all-reduce = (f32[8,3,128]{2,1,0:T(4,128)S(1)}, f32[8,3,128]{2,1,0:T(4,128)S(1)}) all-reduce(f32[8,3,128]{2,1,0:T(4,128)S(1)} %get-tuple-element.6, f32[8,3,128]{2,1,0:T(4,128)S(1)} %get-tuple-element.5), channel_id=1, replica_groups=mesh['wn'=4,'sp'=8] {'sp'}, use_global_device_ids=true, to_apply=%region_4.5 | all-reduce | flops 6144 | bytes 49152 | tf_op jit(solution)/shard_map/psum | solution.py:86
  94.5 0.0 copy-start.2
  94.5 0.2 subtract_divide_fusion
  94.7 0.4 copy-done.2
  95.1 0.2 multiply_add_fusion.1
  95.3 0.1 pad_maximum_fusion.2
  95.5 1.6 %copy.15 = f32[8,3,128,128]{3,2,1,0:T(8,128)} copy(f32[8,3,128,128]{2,3,1,0:T(8,128)S(1)} %pad_maximum_fusion.2) | data formatting | bytes 3145728 | tf_op jit(solution)/shard_map/stack | solution.py:77
  (4 shorter events, 0.1 us)
Async XLA Ops:
  0.0 11.7 %copy-start = (f32[8,3,128,128]{3,2,1,0:T(8,128)S(1)}, f32[8,3,128,128]{3,2,1,0:T(8,128)}, u32[]{:S(2)}) copy-start(f32[8,3,128,128]{3,2,1,0:T(8,128)} %param.3) | copy-start | bytes 4718596
  2.8 5.1 %collective-permute-start = (f32[8,3,64,128]{3,2,1,0:T(8,128)}, f32[8,3,64,128]{3,2,1,0:T(8,128)S(1)}, u32[]{:S(2)}, u32[]{:S(2)}) collective-permute-start(f32[8,3,64,128]{3,2,1,0:T(8,128)} %get-tuple-element.18), channel_id=1, source_target_pairs={{0,8},{8,16},{16,24},{1,9},{9,17},{17,25},{2,10},{10,18},{18,26},{... | collective-permute-start | bytes 2359304 | tf_op jit(solution)/shard_map/ppermute | solution.py:19
  5.2 6.5 %collective-permute-start.1 = (f32[8,3,64,128]{3,2,1,0:T(8,128)}, f32[8,3,64,128]{3,2,1,0:T(8,128)S(1)}, u32[]{:S(2)}, u32[]{:S(2)}) collective-permute-start(f32[8,3,64,128]{3,2,1,0:T(8,128)} %get-tuple-element.19), channel_id=1, source_target_pairs={{8,0},{16,8},{24,16},{9,1},{17,9},{25,17},{10,2},{18,10},{26,18},{... | collective-permute-start | bytes 2359304 | tf_op jit(solution)/shard_map/ppermute | solution.py:22
  17.2 5.0 %copy-start.1 = (f32[6,128]{1,0:T(8,128)S(1)}, f32[6,128]{1,0:T(8,128)}, u32[]{:S(2)}) copy-start(f32[6,128]{1,0:T(8,128)} %param.4) | copy-start | bytes 9220
  17.4 33.7 %collective-permute-start.2 = (f32[8,3,128,64]{2,3,1,0:T(8,128)S(1)}, f32[8,3,128,64]{2,3,1,0:T(8,128)S(1)}, u32[]{:S(2)}, u32[]{:S(2)}) collective-permute-start(f32[8,3,128,64]{2,3,1,0:T(8,128)S(1)} %get-tuple-element.16), channel_id=1, source_target_pairs={{0,1},{1,2},{2,3},{3,4},{4,5},{5,6},{6,7},{7,0},{8,9},{9,10},{10,1... | collective-permute-start | bytes 2359304 | tf_op jit(solution)/shard_map/ppermute | solution.py:19
  19.0 35.9 %collective-permute-start.3 = (f32[8,3,128,64]{2,3,1,0:T(8,128)S(1)}, f32[8,3,128,64]{2,3,1,0:T(8,128)S(1)}, u32[]{:S(2)}, u32[]{:S(2)}) collective-permute-start(f32[8,3,128,64]{2,3,1,0:T(8,128)S(1)} %get-tuple-element.17), channel_id=1, source_target_pairs={{1,0},{2,1},{3,2},{4,3},{5,4},{6,5},{7,6},{0,7},{9,8},{10,9},{11,1... | collective-permute-start | bytes 2359304 | tf_op jit(solution)/shard_map/ppermute | solution.py:22
  94.5 0.7 copy-start.2
where the time goes:
time: 97.3 us; the launch traced here: 97.1 us
  waiting for transfers between devices  36.4 us (37%)
  blocking collectives  35.9 us (37%)
  matrix products  8.62 us (9%)
  starting transfers between devices  8.46 us (9%)
  local copies, waits for them, and re-layouts  5.06 us (5%)
  other arithmetic  1.83 us (2%)
    psum x1, blocking collectives, body(): lax.psum((jnp.sum(filtered, axis=-1), jnp.sum(filtered * filtered, axis=-...  35.9 us
    ppermute x2, waiting for transfers between devices, with_halo(): lax.ppermute(lax.slice_in_dim(block, block.shape[dim] - width, None, axis...  28.9 us
    ppermute x2, waiting for transfers between devices, with_halo(): lax.ppermute(lax.slice_in_dim(block, 0, width, axis=dim), axis, backward)  7.5 us
    ppermute x2, starting transfers between devices, with_halo(): lax.ppermute(lax.slice_in_dim(block, 0, width, axis=dim), axis, backward)  4.52 us
    ppermute x2, starting transfers between devices, with_halo(): lax.ppermute(lax.slice_in_dim(block, block.shape[dim] - width, None, axis...  3.94 us
    slice x2, local copies, waits for them, and re-layouts, with_halo(): lax.slice_in_dim(block, block.shape[dim] - width, None, axis=dim)  2.98 us
    dot_general x1, matrix products, filter_rows(): jnp.einsum('scbjz,ji->scbiz', blocks[:, :, 1:], band[width:], precision=l...  2.66 us
    dot_general x1, matrix products, filter_rows(): jnp.einsum('scbjz,ji->scbiz', blocks[:, :, :-1], band[:width], precision=...  2.63 us
  transfers between devices with their start and end apart: 4, of which 3 were waited for; matrix products, arithmetic and copies ran while one was open for 1% of the time, Pallas kernels for 0%

commit v1 on v0

v1 whole, which is shorter than its diff:
```python
import functools

import jax
import jax.numpy as jnp
from jax import lax
from jax.experimental import pallas as pl
from jax.experimental.pallas import tpu as pltpu
from jax.sharding import PartitionSpec as P

H = 64
LAG = 2

epsilon = 1e-06
MESH = pl.DeviceIdType.MESH
HIGHEST = lax.Precision.HIGHEST


def filter_values(lag, norming):
    scale_len = H / 2.0
    values = jnp.exp(-jnp.pi * lag * lag / (2.0 * scale_len * scale_len)) / norming
    return jnp.where(jnp.abs(lag) <= H, values, 0.0)


def norming_of():
    shape = (-(-(2 * H + 1) // 1024) * 8, 128)
    index = (
        lax.broadcasted_iota(jnp.int32, shape, 0) * 128 + lax.broadcasted_iota(jnp.int32, shape, 1)
    )
    offset = (index - H).astype(jnp.float32)
    scale_len = H / 2.0
    squares = jnp.exp(-jnp.pi * offset * offset / (scale_len * scale_len))
    squares = jnp.where(index <= 2 * H, squares, 0.0)
    return jnp.sqrt(jnp.sum(jnp.sum(squares, axis=1, keepdims=True), axis=0, keepdims=True))


def kernel(
    wn_n, sp_n, x_ref, stress_ref, profile_ref, out_ref,
    padded, normal, to_left, to_right, from_left, from_right, filt, stats, outbuf,
    row_band, span_band, chol,
    load_sem, store_sem, wn_send, wn_recv, sp_send, sp_recv, st_send, st_recv,
):
    steps_n, comps, rows, cols = x_ref.shape
    wn = lax.axis_index("wn")
    me = lax.axis_index("sp")
    left, right = lax.rem(me + sp_n - 1, sp_n), lax.rem(me + 1, sp_n)

    def load(s):
        return pltpu.make_async_copy(
            x_ref.at[s], padded.at[s, :, pl.ds(H, rows)], load_sem.at[s]
        )

    for s in range(steps_n):
        load(s).start()

    barrier = pltpu.get_barrier_semaphore()

    def greet(d, carry):
        pl.semaphore_signal(
            barrier, inc=1, device_id={"sp": lax.rem(me + d, sp_n)}, device_id_type=MESH
        )
        return carry

    lax.fori_loop(1, sp_n, greet, 0)

    @pl.when(wn > 0)
    def _():
        pl.semaphore_signal(barrier, inc=1, device_id={"wn": wn - 1}, device_id_type=MESH)

    @pl.when(wn < wn_n - 1)
    def _():
        pl.semaphore_signal(barrier, inc=1, device_id={"wn": wn + 1}, device_id_type=MESH)

    norming = norming_of()
    target = lax.broadcasted_iota(jnp.int32, (rows, 2 * rows), 0)
    source = lax.broadcasted_iota(jnp.int32, (rows, 2 * rows), 1)
    row_band[...] = filter_values((source - target - H).astype(jnp.float32), norming)
    source = lax.broadcasted_iota(jnp.int32, (2 * cols, cols), 0)
    target = lax.broadcasted_iota(jnp.int32, (2 * cols, cols), 1)
    place = jnp.where(
        source < cols, source, jnp.where(source < cols + H, source - cols - H, source - H)
    )
    span_band[...] = filter_values((place - target).astype(jnp.float32), norming)

    r = [stress_ref[pl.ds(i, 1), :] for i in range(6)]
    a11 = jnp.sqrt(r[0])
    a21 = r[3] / a11
    a22 = jnp.sqrt(r[1] - a21 * a21)
    a31 = r[4] / a11
    a32 = (r[5] - a21 * a31) / a22
    a33 = jnp.sqrt(r[2] - a31 * a31 - a32 * a32)
    for i, a in enumerate((a11, a21, a22, a31, a32, a33, profile_ref[...])):
        chol[pl.ds(i, 1), :] = a

    @pl.when(wn == 0)
    def _():
        padded[:, :, pl.ds(0, H)] = jnp.zeros((steps_n, comps, H, cols), jnp.float32)

    @pl.when(wn == wn_n - 1)
    def _():
        padded[:, :, pl.ds(H + rows, H)] = jnp.zeros((steps_n, comps, H, cols), jnp.float32)

    pl.semaphore_wait(
        barrier, sp_n - 1 + (wn > 0).astype(jnp.int32) + (wn < wn_n - 1).astype(jnp.int32)
    )

    def rows_down(s):
        return pltpu.make_async_remote_copy(
            src_ref=x_ref.at[s, :, pl.ds(0, H)],
            dst_ref=padded.at[s, :, pl.ds(H + rows, H)],
            send_sem=wn_send.at[0, s], recv_sem=wn_recv.at[0, s],
            device_id={"wn": wn - 1}, device_id_type=MESH,
        )

    def rows_up(s):
        return pltpu.make_async_remote_copy(
            src_ref=x_ref.at[s, :, pl.ds(rows - H, H)],
            dst_ref=padded.at[s, :, pl.ds(0, H)],
            send_sem=wn_send.at[1, s], recv_sem=wn_recv.at[1, s],
            device_id={"wn": wn + 1}, device_id_type=MESH,
        )

    def send_rows(s, carry):
        @pl.when(wn > 0)
        def _():
            rows_down(s).start()

        @pl.when(wn < wn_n - 1)
        def _():
            rows_up(s).start()

        return carry

    lax.fori_loop(0, steps_n, send_rows, 0)

    def cols_left(s):
        return pltpu.make_async_remote_copy(
            src_ref=to_left.at[s], dst_ref=from_right.at[s],
            send_sem=sp_send.at[0, s], recv_sem=sp_recv.at[0, s],
            device_id={"sp": left}, device_id_type=MESH,
        )

    def cols_right(s):
        return pltpu.make_async_remote_copy(
            src_ref=to_right.at[s], dst_ref=from_left.at[s],
            send_sem=sp_send.at[1, s], recv_sem=sp_recv.at[1, s],
            device_id={"sp": right}, device_id_type=MESH,
        )

    low_lanes = lax.broadcasted_iota(jnp.int32, (H, cols), 1) < H

    def row_phase(s, carry):
        load(s).wait()

        @pl.when(wn < wn_n - 1)
        def _():
            rows_down(s).wait_recv()

        @pl.when(wn > 0)
        def _():
            rows_up(s).wait_recv()

        for c in range(comps):
            done = jnp.dot(
                row_band[...], padded[s, c], precision=HIGHEST,
                preferred_element_type=jnp.float32,
            )
            normal[s, c] = done
            top, bottom = done[:H], done[H:]
            to_left[s, c] = jnp.where(low_lanes, top, pltpu.roll(bottom, H, 1))
            to_right[s, c] = jnp.where(low_lanes, pltpu.roll(top, H, 1), bottom)
        cols_left(s).start()
        cols_right(s).start()
        return carry

    lax.fori_loop(0, steps_n, row_phase, 0)

    def stats_copy(s, d):
        return pltpu.make_async_remote_copy(
            src_ref=stats.at[s, me], dst_ref=stats.at[s, me],
            send_sem=st_send.at[s, d], recv_sem=st_recv.at[s, d],
            device_id={"sp": lax.rem(me + d, sp_n)}, device_id_type=MESH,
        )

    lane = lax.broadcasted_iota(jnp.int32, (rows, cols), 1)

    def span_phase(s):
        cols_left(s).wait_recv()
        cols_right(s).wait_recv()
        packed = jnp.zeros((rows, cols), jnp.float32)
        for c in range(comps):
            lows, highs = from_left[s, c], from_right[s, c]
            halo = jnp.concatenate(
                [
                    jnp.where(low_lanes, lows, pltpu.roll(highs, H, 1)),
                    jnp.where(low_lanes, pltpu.roll(lows, H, 1), highs),
                ],
                axis=0,
            )
            done = jnp.dot(
                jnp.concatenate([normal[s, c], halo], axis=1), span_band[...],
                precision=HIGHEST, preferred_element_type=jnp.float32,
            )
            filt[s, c] = done
            mean = jnp.sum(done, axis=1, keepdims=True) / cols
            away = done - mean
            second = jnp.sum(away * away, axis=1, keepdims=True)
            packed = jnp.where(lane == c, mean, packed)
            packed = jnp.where(lane == comps + c, second, packed)
        stats[s, me] = packed.T[:8]

        def send(d, carry):
            stats_copy(s, d).start()
            return carry

        lax.fori_loop(1, sp_n, send, 0)

    def store(s):
        return pltpu.make_async_copy(outbuf.at[s], out_ref.at[s], store_sem.at[s])

    def last_phase(s):
        def receive(d, carry):
            stats_copy(s, d).wait_recv()
            return carry

        lax.fori_loop(1, sp_n, receive, 0)
        parts = stats[s]
        total = jnp.sum(parts, axis=0) / sp_n
        away = parts - total[None]
        between = jnp.sum(away * away, axis=0) / sp_n
        var = total[comps : 2 * comps] / cols + between[:comps]
        inv = 1.0 / jnp.sqrt(var + epsilon)
        mean = total[:comps]
        i0, i1, i2 = inv[0:1], inv[1:2], inv[2:3]
        a = [chol[pl.ds(i, 1), :] for i in range(7)]
        table = [
            mean[0:1], mean[1:2], mean[2:3],
            a[0] * i0, a[1] * i0, a[2] * i1, a[3] * i0, a[4] * i1, a[5] * i2, a[6],
        ]
        sub = lax.broadcasted_iota(jnp.int32, (16, rows), 0)
        stacked = jnp.zeros((16, rows), jnp.float32)
        for k, v in enumerate(table):
            stacked = jnp.where(sub == k, v, stacked)
        turned = jnp.concatenate([stacked, jnp.zeros((rows - 16, rows), jnp.float32)], axis=0).T
        col = [turned[:, k : k + 1] for k in range(len(table))]
        d0 = filt[s, 0] - col[0]
        d1 = filt[s, 1] - col[1]
        d2 = filt[s, 2] - col[2]
        outbuf[s, 0] = col[9] + col[3] * d0
        outbuf[s, 1] = col[4] * d0 + col[5] * d1
        outbuf[s, 2] = col[6] * d0 + col[7] * d1 + col[8] * d2
        store(s).start()

    def both(s, carry):
        @pl.when(s < steps_n)
        def _():
            span_phase(s)

        @pl.when(s >= LAG)
        def _():
            last_phase(s - LAG)

        return carry

    lax.fori_loop(0, steps_n + LAG, both, 0)

    def finish(s, carry):
        @pl.when(wn > 0)
        def _():
            rows_down(s).wait_send()

        @pl.when(wn < wn_n - 1)
        def _():
            rows_up(s).wait_send()

        cols_left(s).wait_send()
        cols_right(s).wait_send()

        def sent(d, inner):
            stats_copy(s, d).wait_send()
            return inner

        lax.fori_loop(1, sp_n, sent, 0)
        store(s).wait()
        return carry

    lax.fori_loop(0, steps_n, finish, 0)


def body(random_slabs, stress, profile):
    steps_n, comps, rows, cols = random_slabs.shape
    assert rows == 2 * H and cols == 2 * H and comps == 3
    wn_n, sp_n = lax.axis_size("wn"), lax.axis_size("sp")
    f32 = jnp.float32
    half = (steps_n, comps, H, cols)
    return pl.pallas_call(
        functools.partial(kernel, wn_n, sp_n),
        out_shape=jax.ShapeDtypeStruct(random_slabs.shape, f32),
        in_specs=[
            pl.BlockSpec(memory_space=pl.ANY),
            pl.BlockSpec(memory_space=pltpu.VMEM),
            pl.BlockSpec(memory_space=pltpu.VMEM),
        ],
        out_specs=pl.BlockSpec(memory_space=pl.ANY),
        scratch_shapes=[
            pltpu.VMEM((steps_n, comps, 2 * rows, cols), f32),
            pltpu.VMEM((steps_n, comps, rows, cols), f32),
            pltpu.VMEM(half, f32),
            pltpu.VMEM(half, f32),
            pltpu.VMEM(half, f32),
            pltpu.VMEM(half, f32),
            pltpu.VMEM((steps_n, comps, rows, cols), f32),
            pltpu.VMEM((steps_n, sp_n, 8, rows), f32),
            pltpu.VMEM((steps_n, comps, rows, cols), f32),
            pltpu.VMEM((rows, 2 * rows), f32),
            pltpu.VMEM((2 * cols, cols), f32),
            pltpu.VMEM((8, rows), f32),
            pltpu.SemaphoreType.DMA((steps_n,)),
            pltpu.SemaphoreType.DMA((steps_n,)),
            pltpu.SemaphoreType.DMA((2, steps_n)),
            pltpu.SemaphoreType.DMA((2, steps_n)),
            pltpu.SemaphoreType.DMA((2, steps_n)),
            pltpu.SemaphoreType.DMA((2, steps_n)),
            pltpu.SemaphoreType.DMA((steps_n, sp_n)),
            pltpu.SemaphoreType.DMA((steps_n, sp_n)),
        ],
        compiler_params=pltpu.CompilerParams(
            collective_id=0, has_side_effects=True, vmem_limit_bytes=40 * 2**20
        ),
    )(random_slabs, stress, profile.reshape(1, rows))


def solution(mesh):
    return jax.shard_map(
        body,
        mesh=mesh,
        in_specs=(P(None, None, "wn", "sp"), P(None, "wn"), P("wn")),
        out_specs=P(None, None, "wn", "sp"),
        check_vma=False,
    )
```

time: 97.3 us -> 63.6 us (0.65)
  Pallas kernels: 0 us -> 59.5 us
  waiting for transfers between devices: 36.4 us -> 0 us
  blocking collectives: 35.9 us -> 0 us
  matrix products: 8.62 us -> 0 us
  starting transfers between devices: 8.46 us -> 0 us
  other arithmetic: 1.83 us -> 0 us
  local copies, waits for them, and re-layouts: 5.06 us -> 3.89 us
    pallas_call x0 -> x1, Pallas kernels: none -> 59.5 us  [body(): pl.pallas_call(functools.partial(kernel, wn_n, sp_n), out_shape=jax.Shape...]
    ppermute x4 -> x0, waiting for transfers between devices: 36.4 us -> none  [the longest x2 28.9 us: with_halo(): lax.ppermute(lax.slice_in_dim(block, block.shape[dim] - width, None, axis...]
    psum x1 -> x0, blocking collectives: 35.9 us -> none  [body(): lax.psum((jnp.sum(filtered, axis=-1), jnp.sum(filtered * filtered, axis=-...]
    dot_general x4 -> x0, matrix products: 8.62 us -> none  [the longest x1 2.66 us: filter_rows(): jnp.einsum('scbjz,ji->scbiz', blocks[:, :, 1:], band[width:], precision=l...]
    ppermute x4 -> x0, starting transfers between devices: 8.46 us -> none  [the longest x2 4.52 us: with_halo(): lax.ppermute(lax.slice_in_dim(block, 0, width, axis=dim), axis, backward)]
    unnamed x6 -> x7, local copies, waits for them, and re-layouts: 0.46 us -> 3.89 us
    slice x2 -> x0, local copies, waits for them, and re-layouts: 2.98 us -> none  [with_halo(): lax.slice_in_dim(block, block.shape[dim] - width, None, axis=dim)]
    another operation x1 -> x0, local copies, waits for them, and re-layouts: 1.62 us -> none  [lund(): return jnp.stack([first, second, third], axis=1)]
  transfers between devices with their start and end apart: 4 -> 0, of which waited for: 3 -> 0; matrix products, arithmetic and copies ran while one was open for 1% -> 0% of each run, Pallas kernels for 0% -> 0%
where the time goes in v1:
time: 63.6 us; the launch traced here: 63.4 us
  Pallas kernels  59.5 us (94%)
  local copies, waits for them, and re-layouts  3.89 us (6%)
    pallas_call x1, Pallas kernels, body(): pl.pallas_call(functools.partial(kernel, wn_n, sp_n), out_shape=jax.Shape...  59.5 us
    unnamed x7, local copies, waits for them, and re-layouts  3.89 us

profile of v1, /device:TPU:0, one launch (start us, length us, event | category | flops | bytes accessed | tf_op | source)
XLA Modules:
  0.0 63.4 jit_solution(13513119698070100461)
XLA Ops:
  0.0 0.0 copy-start
  0.0 1.4 %copy-done = f32[8,3,128,128]{3,2,1,0:T(8,128)S(1)} copy-done((f32[8,3,128,128]{3,2,1,0:T(8,128)S(1)}, f32[8,3,128,128]{3,2,1,0:T(8,128)}, u32[]{:S(2)}) %copy-start) | copy-done | bytes 1572888
  1.4 0.0 copy-start.1
  1.4 0.7 %copy-done.1 = f32[6,128]{1,0:T(8,128)S(1)} copy-done((f32[6,128]{1,0:T(8,128)S(1)}, f32[6,128]{1,0:T(8,128)}, u32[]{:S(2)}) %copy-start.1) | copy-done | bytes 3096
  2.1 0.0 copy-start.2
  2.1 0.7 %copy-done.2 = f32[128]{0:T(128)S(1)} copy-done((f32[128]{0:T(128)S(1)}, f32[128]{0:T(128)}, u32[]{:S(2)}) %copy-start.2) | copy-done | bytes 536
  2.8 59.5 %shard_map.37 = f32[8,3,128,128]{3,2,1,0:T(8,128)S(1)} custom-call(f32[8,3,128,128]{3,2,1,0:T(8,128)S(1)} %copy-done, f32[6,128]{1,0:T(8,128)S(1)} %copy-done.1, f32[1,128]{1,0:T(1,128)S(1)} %bitcast.1), custom_call_target="tpu_custom_call" | custom-call | tf_op jit(solution)/shard_map/pallas_call | solution.py:295
  62.3 1.1 %copy.5 = f32[8,3,128,128]{3,2,1,0:T(8,128)} copy(f32[8,3,128,128]{3,2,1,0:T(8,128)S(1)} %shard_map.37) | data formatting | bytes 3145728
Async XLA Ops:
  0.0 1.4 %copy-start = (f32[8,3,128,128]{3,2,1,0:T(8,128)S(1)}, f32[8,3,128,128]{3,2,1,0:T(8,128)}, u32[]{:S(2)}) copy-start(f32[8,3,128,128]{3,2,1,0:T(8,128)} %x_ref.1) | copy-start | bytes 4718596
  1.4 0.7 %copy-start.1 = (f32[6,128]{1,0:T(8,128)S(1)}, f32[6,128]{1,0:T(8,128)}, u32[]{:S(2)}) copy-start(f32[6,128]{1,0:T(8,128)} %stress_ref.1) | copy-start | bytes 9220
  2.1 0.7 %copy-start.2 = (f32[128]{0:T(128)S(1)}, f32[128]{0:T(128)}, u32[]{:S(2)}) copy-start(f32[128]{0:T(128)} %param.5) | copy-start | bytes 1540

commit v2 on v1

--- a/solution.py
+++ b/solution.py
@@ -8,6 +8,7 @@
 from jax.sharding import PartitionSpec as P
 
 H = 64
+FIRST = 2
 LAG = 2
 
 epsilon = 1e-06
@@ -34,16 +35,24 @@
 
 
 def kernel(
-    wn_n, sp_n, x_ref, stress_ref, profile_ref, out_ref,
-    padded, normal, to_left, to_right, from_left, from_right, filt, stats, outbuf,
+    wn_n, sp_n, x_ref, stress_hbm, profile_hbm, out_ref,
+    stress_ref, profile_ref, padded, normal, to_left, to_right, from_left, from_right, filt, stats, outbuf,
     row_band, span_band, chol,
-    load_sem, store_sem, wn_send, wn_recv, sp_send, sp_recv, st_send, st_recv,
+    load_sem, small_sem, store_sem, wn_send, wn_recv, sp_send, sp_recv, st_send, st_recv,
 ):
     steps_n, comps, rows, cols = x_ref.shape
     wn = lax.axis_index("wn")
     me = lax.axis_index("sp")
     left, right = lax.rem(me + sp_n - 1, sp_n), lax.rem(me + 1, sp_n)
 
+    barrier = pltpu.get_barrier_semaphore()
+
+    def greet(d, carry):
+        pl.semaphore_signal(
+            barrier, inc=1, device_id={"sp": lax.rem(me + d, sp_n)}, device_id_type=MESH
+        )
+        return carry
+
     def load(s):
         return pltpu.make_async_copy(
             x_ref.at[s], padded.at[s, :, pl.ds(H, rows)], load_sem.at[s]
@@ -51,14 +60,12 @@
 
     for s in range(steps_n):
         load(s).start()
-
-    barrier = pltpu.get_barrier_semaphore()
-
-    def greet(d, carry):
-        pl.semaphore_signal(
-            barrier, inc=1, device_id={"sp": lax.rem(me + d, sp_n)}, device_id_type=MESH
-        )
-        return carry
+    smalls = [
+        pltpu.make_async_copy(stress_hbm, stress_ref, small_sem.at[0]),
+        pltpu.make_async_copy(profile_hbm, profile_ref, small_sem.at[1]),
+    ]
+    for small in smalls:
+        small.start()
 
     lax.fori_loop(1, sp_n, greet, 0)
 
@@ -69,6 +76,92 @@
     @pl.when(wn < wn_n - 1)
     def _():
         pl.semaphore_signal(barrier, inc=1, device_id={"wn": wn + 1}, device_id_type=MESH)
+
+    low_lanes = lax.broadcasted_iota(jnp.int32, (H, cols), 1) < H
+
+    def pack(s, c, tile):
+        top, bottom = tile[:H], tile[H:]
+        to_left[s, c] = jnp.where(low_lanes, top, pltpu.roll(bottom, H, 1))
+        to_right[s, c] = jnp.where(low_lanes, pltpu.roll(top, H, 1), bottom)
+
+    def halo_of(s, c):
+        lows, highs = from_left[s, c], from_right[s, c]
+        return jnp.concatenate(
+            [
+                jnp.where(low_lanes, lows, pltpu.roll(highs, H, 1)),
+                jnp.where(low_lanes, pltpu.roll(lows, H, 1), highs),
+            ],
+            axis=0,
+        )
+
+    for s in range(FIRST):
+        load(s).wait()
+        for c in range(comps):
+            pack(s, c, padded[s, c, pl.ds(H, rows)])
+
+    pl.semaphore_wait(
+        barrier, sp_n - 1 + (wn > 0).astype(jnp.int32) + (wn < wn_n - 1).astype(jnp.int32)
+    )
+
+    def cols_left(s):
+        return pltpu.make_async_remote_copy(
+            src_ref=to_left.at[s], dst_ref=from_right.at[s],
+            send_sem=sp_send.at[0, s], recv_sem=sp_recv.at[0, s],
+            device_id={"sp": left}, device_id_type=MESH,
+        )
+
+    def cols_right(s):
+        return pltpu.make_async_remote_copy(
+            src_ref=to_right.at[s], dst_ref=from_left.at[s],
+            send_sem=sp_send.at[1, s], recv_sem=sp_recv.at[1, s],
+            device_id={"sp": right}, device_id_type=MESH,
+        )
+
+    for s in range(FIRST):
+        cols_left(s).start()
+        cols_right(s).start()
+
+    def rows_down(s, filtered=False):
+        return pltpu.make_async_remote_copy(
+            src_ref=padded.at[s, :, pl.ds(H, H)] if filtered else x_ref.at[s, :, pl.ds(0, H)],
+            dst_ref=padded.at[s, :, pl.ds(H + rows, H)],
+            send_sem=wn_send.at[0, s], recv_sem=wn_recv.at[0, s],
+            device_id={"wn": wn - 1}, device_id_type=MESH,
+        )
+
+    def rows_up(s, filtered=False):
+        return pltpu.make_async_remote_copy(
+            src_ref=padded.at[s, :, pl.ds(rows, H)]
+            if filtered
+            else x_ref.at[s, :, pl.ds(rows - H, H)],
+            dst_ref=padded.at[s, :, pl.ds(0, H)],
+            send_sem=wn_send.at[1, s], recv_sem=wn_recv.at[1, s],
+            device_id={"wn": wn + 1}, device_id_type=MESH,
+        )
+
+    def send_rows(s, filtered):
+        @pl.when(wn > 0)
+        def _():
+            rows_down(s, filtered).start()
+
+        @pl.when(wn < wn_n - 1)
+        def _():
+            rows_up(s, filtered).start()
+
+    def receive_rows(s):
+        @pl.when(wn < wn_n - 1)
+        def _():
+            rows_down(s).wait_recv()
+
+        @pl.when(wn > 0)
+        def _():
+            rows_up(s).wait_recv()
+
+    def send_later_rows(s, carry):
+        send_rows(s, False)
+        return carry
+
+    lax.fori_loop(FIRST, steps_n, send_later_rows, 0)
 
     norming = norming_of()
     target = lax.broadcasted_iota(jnp.int32, (rows, 2 * rows), 0)
@@ -81,6 +174,52 @@
     )
     span_band[...] = filter_values((place - target).astype(jnp.float32), norming)
 
+    @pl.when(wn == 0)
+    def _():
+        padded[:, :, pl.ds(0, H)] = jnp.zeros((steps_n, comps, H, cols), jnp.float32)
+
+    @pl.when(wn == wn_n - 1)
+    def _():
+        padded[:, :, pl.ds(H + rows, H)] = jnp.zeros((steps_n, comps, H, cols), jnp.float32)
+
+    def filter_rows(s, c):
+        return jnp.dot(
+            row_band[...], padded[s, c], precision=HIGHEST, preferred_element_type=jnp.float32
+        )
+
+    def filter_cols(tile, halo):
+        return jnp.dot(
+            jnp.concatenate([tile, halo], axis=1), span_band[...],
+            precision=HIGHEST, preferred_element_type=jnp.float32,
+        )
+
+    def row_phase(s, carry):
+        load(s).wait()
+        receive_rows(s)
+        for c in range(comps):
+            done = filter_rows(s, c)
+            normal[s, c] = done
+            pack(s, c, done)
+        cols_left(s).start()
+        cols_right(s).start()
+        return carry
+
+    lax.fori_loop(FIRST, steps_n, row_phase, 0)
+
+    def first_span_phase(s, carry):
+        cols_left(s).wait_recv()
+        cols_right(s).wait_recv()
+        for c in range(comps):
+            padded[s, c, pl.ds(H, rows)] = filter_cols(
+                padded[s, c, pl.ds(H, rows)], halo_of(s, c)
+            )
+        send_rows(s, True)
+        return carry
+
+    lax.fori_loop(0, FIRST, first_span_phase, 0)
+
+    for small in smalls:
+        small.wait()
     r = [stress_ref[pl.ds(i, 1), :] for i in range(6)]
     a11 = jnp.sqrt(r[0])
     a21 = r[3] / a11
@@ -91,89 +230,6 @@
     for i, a in enumerate((a11, a21, a22, a31, a32, a33, profile_ref[...])):
         chol[pl.ds(i, 1), :] = a
 
-    @pl.when(wn == 0)
-    def _():
-        padded[:, :, pl.ds(0, H)] = jnp.zeros((steps_n, comps, H, cols), jnp.float32)
-
-    @pl.when(wn == wn_n - 1)
-    def _():
-        padded[:, :, pl.ds(H + rows, H)] = jnp.zeros((steps_n, comps, H, cols), jnp.float32)
-
-    pl.semaphore_wait(
-        barrier, sp_n - 1 + (wn > 0).astype(jnp.int32) + (wn < wn_n - 1).astype(jnp.int32)
-    )
-
-    def rows_down(s):
-        return pltpu.make_async_remote_copy(
-            src_ref=x_ref.at[s, :, pl.ds(0, H)],
-            dst_ref=padded.at[s, :, pl.ds(H + rows, H)],
-            send_sem=wn_send.at[0, s], recv_sem=wn_recv.at[0, s],
-            device_id={"wn": wn - 1}, device_id_type=MESH,
-        )
-
-    def rows_up(s):
-        return pltpu.make_async_remote_copy(
-            src_ref=x_ref.at[s, :, pl.ds(rows - H, H)],
-            dst_ref=padded.at[s, :, pl.ds(0, H)],
-            send_sem=wn_send.at[1, s], recv_sem=wn_recv.at[1, s],
-            device_id={"wn": wn + 1}, device_id_type=MESH,
-        )
-
-    def send_rows(s, carry):
-        @pl.when(wn > 0)
-        def _():
-            rows_down(s).start()
-
-        @pl.when(wn < wn_n - 1)
-        def _():
-            rows_up(s).start()
-
-        return carry
-
-    lax.fori_loop(0, steps_n, send_rows, 0)
-
-    def cols_left(s):
-        return pltpu.make_async_remote_copy(
-            src_ref=to_left.at[s], dst_ref=from_right.at[s],
-            send_sem=sp_send.at[0, s], recv_sem=sp_recv.at[0, s],
-            device_id={"sp": left}, device_id_type=MESH,
-        )
-
-    def cols_right(s):
-        return pltpu.make_async_remote_copy(
-            src_ref=to_right.at[s], dst_ref=from_left.at[s],
-            send_sem=sp_send.at[1, s], recv_sem=sp_recv.at[1, s],
-            device_id={"sp": right}, device_id_type=MESH,
-        )
-
-    low_lanes = lax.broadcasted_iota(jnp.int32, (H, cols), 1) < H
-
-    def row_phase(s, carry):
-        load(s).wait()
-
-        @pl.when(wn < wn_n - 1)
-        def _():
-            rows_down(s).wait_recv()
-
-        @pl.when(wn > 0)
-        def _():
-            rows_up(s).wait_recv()
-
-        for c in range(comps):
-            done = jnp.dot(
-                row_band[...], padded[s, c], precision=HIGHEST,
-                preferred_element_type=jnp.float32,
-            )
-            normal[s, c] = done
-            top, bottom = done[:H], done[H:]
-            to_left[s, c] = jnp.where(low_lanes, top, pltpu.roll(bottom, H, 1))
-            to_right[s, c] = jnp.where(low_lanes, pltpu.roll(top, H, 1), bottom)
-        cols_left(s).start()
-        cols_right(s).start()
-        return carry
-
-    lax.fori_loop(0, steps_n, row_phase, 0)
-
     def stats_copy(s, d):
         return pltpu.make_async_remote_copy(
             src_ref=stats.at[s, me], dst_ref=stats.at[s, me],
@@ -183,23 +239,10 @@
 
     lane = lax.broadcasted_iota(jnp.int32, (rows, cols), 1)
 
-    def span_phase(s):
-        cols_left(s).wait_recv()
-        cols_right(s).wait_recv()
+    def publish(s, tile_of):
         packed = jnp.zeros((rows, cols), jnp.float32)
         for c in range(comps):
-            lows, highs = from_left[s, c], from_right[s, c]
-            halo = jnp.concatenate(
-                [
-                    jnp.where(low_lanes, lows, pltpu.roll(highs, H, 1)),
-                    jnp.where(low_lanes, pltpu.roll(lows, H, 1), highs),
-                ],
-                axis=0,
-            )
-            done = jnp.dot(
-                jnp.concatenate([normal[s, c], halo], axis=1), span_band[...],
-                precision=HIGHEST, preferred_element_type=jnp.float32,
-            )
+            done = tile_of(c)
             filt[s, c] = done
             mean = jnp.sum(done, axis=1, keepdims=True) / cols
             away = done - mean
@@ -213,6 +256,15 @@
             return carry
 
         lax.fori_loop(1, sp_n, send, 0)
+
+    def span_phase(s):
+        cols_left(s).wait_recv()
+        cols_right(s).wait_recv()
+        publish(s, lambda c: filter_cols(normal[s, c], halo_of(s, c)))
+
+    def first_row_phase(s):
+        receive_rows(s)
+        publish(s, lambda c: filter_rows(s, c))
 
     def store(s):
         return pltpu.make_async_copy(outbuf.at[s], out_ref.at[s], store_sem.at[s])
@@ -255,13 +307,21 @@
         def _():
             span_phase(s)
 
-        @pl.when(s >= LAG)
+        @pl.when(s < 2 * FIRST)
+        def _():
+            first_row_phase(s - FIRST)
+
+        @pl.when(s >= FIRST + LAG)
         def _():
             last_phase(s - LAG)
 
-        return carry
-
-    lax.fori_loop(0, steps_n + LAG, both, 0)
+        @pl.when((s >= FIRST + LAG) & (s < 2 * FIRST + LAG))
+        def _():
+            last_phase(s - FIRST - LAG)
+
+        return carry
+
+    lax.fori_loop(FIRST, steps_n + LAG, both, 0)
 
     def finish(s, carry):
         @pl.when(wn > 0)
@@ -295,13 +355,11 @@
     return pl.pallas_call(
         functools.partial(kernel, wn_n, sp_n),
         out_shape=jax.ShapeDtypeStruct(random_slabs.shape, f32),
-        in_specs=[
-            pl.BlockSpec(memory_space=pl.ANY),
-            pl.BlockSpec(memory_space=pltpu.VMEM),
-            pl.BlockSpec(memory_space=pltpu.VMEM),
-        ],
+        in_specs=[pl.BlockSpec(memory_space=pltpu.HBM)] * 3,
         out_specs=pl.BlockSpec(memory_space=pl.ANY),
         scratch_shapes=[
+            pltpu.VMEM((6, rows), f32),
+            pltpu.VMEM((1, rows), f32),
             pltpu.VMEM((steps_n, comps, 2 * rows, cols), f32),
             pltpu.VMEM((steps_n, comps, rows, cols), f32),
             pltpu.VMEM(half, f32),
@@ -315,6 +373,7 @@
             pltpu.VMEM((2 * cols, cols), f32),
             pltpu.VMEM((8, rows), f32),
             pltpu.SemaphoreType.DMA((steps_n,)),
+            pltpu.SemaphoreType.DMA((2,)),
             pltpu.SemaphoreType.DMA((steps_n,)),
             pltpu.SemaphoreType.DMA((2, steps_n)),
             pltpu.SemaphoreType.DMA((2, steps_n)),
@@ -324,7 +383,7 @@
             pltpu.SemaphoreType.DMA((steps_n, sp_n)),
         ],
         compiler_params=pltpu.CompilerParams(
-            collective_id=0, has_side_effects=True, vmem_limit_bytes=40 * 2**20
+            collective_id=0, has_side_effects=True, vmem_limit_bytes=58 * 2**20
         ),
     )(random_slabs, stress, profile.reshape(1, rows))
 

time: 63.6 us -> 56.4 us (0.89)
  Pallas kernels: 59.5 us -> 53.6 us
  local copies, waits for them, and re-layouts: 3.89 us -> 2.7 us
    pallas_call x1, Pallas kernels: 59.5 us -> 53.6 us  [body(): pl.pallas_call(functools.partial(kernel, wn_n, sp_n), out_shape=jax.Shape...]
    unnamed x7 -> x1, local copies, waits for them, and re-layouts: 3.89 us -> 2.7 us
where the time goes in v2:
time: 56.4 us; the launch traced here: 56.3 us
  Pallas kernels  53.6 us (95%)
  local copies, waits for them, and re-layouts  2.7 us (5%)
    pallas_call x1, Pallas kernels, body(): pl.pallas_call(functools.partial(kernel, wn_n, sp_n), out_shape=jax.Shape...  53.6 us
    unnamed x1, local copies, waits for them, and re-layouts  2.7 us

profile of v2, /device:TPU:0, one launch (start us, length us, event | category | flops | bytes accessed | tf_op | source)
XLA Modules:
  0.0 56.3 jit_solution(14023101929431880639)
XLA Ops:
  0.0 53.6 %shard_map.37 = f32[8,3,128,128]{3,2,1,0:T(8,128)} custom-call(f32[8,3,128,128]{3,2,1,0:T(8,128)} %x_ref.1, f32[6,128]{1,0:T(8,128)} %stress_hbm.1, f32[1,128]{1,0:T(1,128)} %bitcast.1), custom_call_target="tpu_custom_call" | custom-call | tf_op jit(solution)/shard_map/pallas_call | solution.py:355
  53.6 2.7 %copy.5 = f32[8,3,128,128]{3,2,1,0:T(8,128)} copy(f32[8,3,128,128]{3,2,1,0:T(8,128)} %shard_map.37) | data formatting | bytes 3145728

commit v3 on v2

--- a/solution.py
+++ b/solution.py
@@ -8,8 +8,8 @@
 from jax.sharding import PartitionSpec as P
 
 H = 64
-FIRST = 2
-LAG = 2
+FIRST = 3
+LAG = 4
 
 epsilon = 1e-06
 MESH = pl.DeviceIdType.MESH
@@ -232,7 +232,8 @@
 
     def stats_copy(s, d):
         return pltpu.make_async_remote_copy(
-            src_ref=stats.at[s, me], dst_ref=stats.at[s, me],
+            src_ref=stats.at[s, me, pl.ds(0, 2 * comps)],
+            dst_ref=stats.at[s, me, pl.ds(0, 2 * comps)],
             send_sem=st_send.at[s, d], recv_sem=st_recv.at[s, d],
             device_id={"sp": lax.rem(me + d, sp_n)}, device_id_type=MESH,
         )
@@ -249,7 +250,7 @@
             second = jnp.sum(away * away, axis=1, keepdims=True)
             packed = jnp.where(lane == c, mean, packed)
             packed = jnp.where(lane == comps + c, second, packed)
-        stats[s, me] = packed.T[:8]
+        stats[s, me, pl.ds(0, 2 * comps)] = packed.T[: 2 * comps]
 
         def send(d, carry):
             stats_copy(s, d).start()
@@ -270,12 +271,29 @@
         return pltpu.make_async_copy(outbuf.at[s], out_ref.at[s], store_sem.at[s])
 
     def last_phase(s):
+        @pl.when(wn > 0)
+        def _():
+            rows_down(s).wait_send()
+
+        @pl.when(wn < wn_n - 1)
+        def _():
+            rows_up(s).wait_send()
+
+        cols_left(s).wait_send()
+        cols_right(s).wait_send()
+
+        def sent(d, inner):
+            stats_copy(s, d).wait_send()
+            return inner
+
+        lax.fori_loop(1, sp_n, sent, 0)
+
         def receive(d, carry):
             stats_copy(s, d).wait_recv()
             return carry
 
         lax.fori_loop(1, sp_n, receive, 0)
-        parts = stats[s]
+        parts = stats[s, :, pl.ds(0, 2 * comps)]
         total = jnp.sum(parts, axis=0) / sp_n
         away = parts - total[None]
         between = jnp.sum(away * away, axis=0) / sp_n
@@ -324,22 +342,6 @@
     lax.fori_loop(FIRST, steps_n + LAG, both, 0)
 
     def finish(s, carry):
-        @pl.when(wn > 0)
-        def _():
-            rows_down(s).wait_send()
-
-        @pl.when(wn < wn_n - 1)
-        def _():
-            rows_up(s).wait_send()
-
-        cols_left(s).wait_send()
-        cols_right(s).wait_send()
-
-        def sent(d, inner):
-            stats_copy(s, d).wait_send()
-            return inner
-
-        lax.fori_loop(1, sp_n, sent, 0)
         store(s).wait()
         return carry
 

time: 56.4 us -> 52.4 us (0.929)
  Pallas kernels: 53.6 us -> 49.6 us
    pallas_call x1, Pallas kernels: 53.6 us -> 49.6 us  [body(): pl.pallas_call(functools.partial(kernel, wn_n, sp_n), out_shape=jax.Shape...]
where the time goes in v3:
time: 52.4 us; the launch traced here: 52.3 us
  Pallas kernels  49.6 us (95%)
  local copies, waits for them, and re-layouts  2.7 us (5%)
    pallas_call x1, Pallas kernels, body(): pl.pallas_call(functools.partial(kernel, wn_n, sp_n), out_shape=jax.Shape...  49.6 us
    unnamed x1, local copies, waits for them, and re-layouts  2.7 us

profile of v3, /device:TPU:0, one launch (start us, length us, event | category | flops | bytes accessed | tf_op | source)
XLA Modules:
  0.0 52.3 jit_solution(16460174811527622542)
XLA Ops:
  0.0 49.6 %shard_map.37 = f32[8,3,128,128]{3,2,1,0:T(8,128)} custom-call(f32[8,3,128,128]{3,2,1,0:T(8,128)} %x_ref.1, f32[6,128]{1,0:T(8,128)} %stress_hbm.1, f32[1,128]{1,0:T(1,128)} %bitcast.1), custom_call_target="tpu_custom_call" | custom-call | tf_op jit(solution)/shard_map/pallas_call | solution.py:357
  49.6 2.7 %copy.5 = f32[8,3,128,128]{3,2,1,0:T(8,128)} copy(f32[8,3,128,128]{3,2,1,0:T(8,128)} %shard_map.37) | data formatting | bytes 3145728
